TPU v7x, 32 devices: a whole 2x2x4 slice. The times are simulated.
32 devices in a mesh: grp: 2 (over y), tok: 4 (over z), fac: 2 (over x), sub: 2 (over core).
Axes of the slice: x: 2, y: 2, z: 4, core: 2. Of those that a mesh axis runs over, the one named last changes fastest.
Arguments:
- activations: bfloat16 [1024, 5120], P(('grp', 'tok')), parts along dimension 0, may hold values from -6 to 6
- gradients: bfloat16 [1024, 13824], P(('grp', 'tok')), parts along dimension 0, may hold values from -6 to 6
- tok_class: int32 [1024, 1], P('grp'), parts along dimension 0, may hold values from 0 to 1; in each aligned block of 64 rows (0 to 63, 64 to 127, ...) at most 40 rows name the same one
- query_inputs: bfloat16 [1024, 5120], P('grp', 'tok'), parts along dimension 0, may hold values from -6 to 6
- query_gradients: bfloat16 [1024, 13824], P('grp', 'tok'), parts along dimension 0, may hold values from -6 to 6
- query_class: int32 [1024, 1], P('grp'), parts along dimension 0, may hold values from 0 to 1; in each aligned block of 256 rows (0 to 255, 256 to 511, ...) at most 160 rows name the same one
- basis_a: bfloat16 [2, 5120, 5120], P(None, 'tok', ('fac', 'sub')), may hold values from -0.078125 to 0.078125
- basis_g: bfloat16 [2, 13824, 13824], P(None, 'tok', ('fac', 'sub')), may hold values from -0.0546875 to 0.0546875
- eigen_a: float32 [2, 5120], P(None, ('fac', 'sub')), may hold values from 0.5 to 8
- eigen_g: float32 [2, 13824], P(None, ('fac', 'sub')), may hold values from 0.5 to 8
Outputs:
- scores: float32 [512, 1024], P('fac', ('grp', 'tok', 'sub')), parts along dimension 1
There are 2 independent parts, one for each index of `grp`. A program takes and returns all parts, laid end to end along the dimension named above; an argument that names none is the same for every part. Nothing has to cross between parts.
Inputs may be any that keep to these rules, and one draw needn't show every extreme that they name: `tok_class`: in each half of the 128 training tokens of one index of tok no class is named by more than 40 tokens, and in every draw some class reaches that. `query_class`: the queries fall into equal blocks in order, one for each index of fac; in each block no class is named by more than 160 queries, and in every draw some class reaches that.
All inputs are finite; a program needn't handle non-finite values.
Results may differ from a plain program's by a relative error of at most 0.0003.
Values may be sent and summed in bfloat16 or wider, within the bound.
No kernel may reach another device: no remote copies, remote signals or barrier semaphores. Data moves between devices by JAX's collectives and lax.ppermute only.
A program may use at most 256 MiB of HBM per device.

v0:
```python
import math

import jax
import jax.numpy as jnp
from jax import lax
from jax.sharding import PartitionSpec as P

D = 5120
FH = 13824


DAMPING = 0.25


def slot_table(ids, classes, slot_cap, kind):
    onehot = ids[..., None, :] == jnp.arange(classes, dtype=jnp.int32)[:, None]
    within = jnp.cumsum(onehot.astype(jnp.int32), axis=-1) - 1
    chosen = onehot[..., :, None, :] & (
        within[..., :, None, :] == jnp.arange(slot_cap, dtype=jnp.int32)[:, None]
    )
    return chosen.astype(kind)


def pack_rows(tables, features):
    packed = jnp.einsum(
        "bcph,bhr->cbpr", tables, features, preferred_element_type=jnp.float32
    ).astype(jnp.bfloat16)
    return packed.reshape(packed.shape[0], packed.shape[1] * packed.shape[2], packed.shape[3])


def body(
    activations,
    gradients,
    tok_class,
    query_inputs,
    query_gradients,
    query_class,
    basis_a,
    basis_g,
    eigen_a,
    eigen_g,
):
    classes = basis_g.shape[0]
    tok_count = lax.axis_size("tok")
    fac_count = lax.axis_size("fac")
    sub_count = lax.axis_size("sub")
    tok_rows = activations.shape[0]
    half_rows = tok_rows // sub_count
    slot_cap = 5 * half_rows // 8
    query_block = query_inputs.shape[0] // fac_count
    query_cap = 5 * query_block // 8
    token_ids = tok_class[:, 0]
    query_ids = query_class[:, 0]
    raw_g, raw_a = (
        lax.all_to_all(gradients, "tok", split_axis=1, concat_axis=0, tiled=True),
        lax.all_to_all(activations, "tok", split_axis=1, concat_axis=0, tiled=True),
    )
    tables = slot_table(
        token_ids.reshape(tok_count * sub_count, half_rows), classes, slot_cap, jnp.bfloat16
    )
    moved_g = pack_rows(tables, raw_g.reshape(tok_count * sub_count, half_rows, raw_g.shape[1]))
    moved_a = pack_rows(tables, raw_a.reshape(tok_count * sub_count, half_rows, raw_a.shape[1]))
    weight_g = 1.0 / (eigen_g + DAMPING)
    weight_a = 1.0 / (eigen_a + DAMPING)
    coords_g = (
        jnp.einsum("csr,crk->csk", moved_g, basis_g, preferred_element_type=jnp.float32)
        * weight_g[:, None, :]
    )
    coords_a = (
        jnp.einsum("csr,crk->csk", moved_a, basis_a, preferred_element_type=jnp.float32)
        * weight_a[:, None, :]
    )
    width_g = coords_g.shape[2]
    width_a = coords_a.shape[2]
    query_tables = slot_table(
        query_ids.reshape(fac_count, query_block), classes, query_cap, jnp.bfloat16
    )
    qpacked_g = jnp.einsum(
        "fcqb,fbr->cfqr",
        query_tables,
        query_gradients.reshape(fac_count, query_block, query_gradients.shape[1]),
        preferred_element_type=jnp.float32,
    ).astype(jnp.bfloat16)
    qpacked_a = jnp.einsum(
        "fcqb,fbr->cfqr",
        query_tables,
        query_inputs.reshape(fac_count, query_block, query_inputs.shape[1]),
        preferred_element_type=jnp.float32,
    ).astype(jnp.bfloat16)
    partial_g = jnp.einsum("cfqr,crk->cfqk", qpacked_g, basis_g, preferred_element_type=jnp.float32)
    partial_a = jnp.einsum("cfqr,crk->cfqk", qpacked_a, basis_a, preferred_element_type=jnp.float32)
    query_g, query_a = lax.psum((partial_g, partial_a), "tok")
    home_g, home_a = (
        lax.psum_scatter(coords_g, "tok", scatter_dimension=1, tiled=True),
        lax.psum_scatter(coords_a, "tok", scatter_dimension=1, tiled=True),
    )
    home_g = home_g.reshape(classes, sub_count, slot_cap, width_g)
    home_a = home_a.reshape(classes, sub_count, slot_cap, width_a)
    pieces_g = jnp.einsum("cfqk,cspk->fscqp", query_g, home_g, precision=lax.Precision.HIGHEST)
    pieces_a = jnp.einsum("cfqk,cspk->fscqp", query_a, home_a, precision=lax.Precision.HIGHEST)
    pieces_g = pieces_g.reshape(fac_count * sub_count, classes, query_cap, slot_cap)
    pieces_a = pieces_a.reshape(fac_count * sub_count, classes, query_cap, slot_cap)
    side_g, side_a = (
        lax.psum_scatter(pieces_g, ("fac", "sub"), scatter_dimension=0, tiled=True),
        lax.psum_scatter(pieces_a, ("fac", "sub"), scatter_dimension=0, tiled=True),
    )
    factor = 1.0 / math.sqrt(FH * D)
    slot_scores = side_g[0] * side_a[0] * factor
    own_queries = lax.dynamic_slice_in_dim(
        query_ids, lax.axis_index("fac") * query_block, query_block
    )
    own_tokens = lax.dynamic_slice_in_dim(
        token_ids, lax.axis_index("tok") * tok_rows + lax.axis_index("sub") * half_rows, half_rows
    )
    query_map = slot_table(own_queries, classes, query_cap, jnp.float32)
    token_map = slot_table(own_tokens, classes, slot_cap, jnp.float32)
    by_query = jnp.einsum("cqb,cqp->cbp", query_map, slot_scores, precision=lax.Precision.HIGHEST)
    return jnp.einsum("cbp,cph->bh", by_query, token_map, precision=lax.Precision.HIGHEST)


def solution(mesh):
    placed = (
        P(("grp", "tok"), None),
        P(("grp", "tok"), None),
        P("grp", None),
        P("grp", "tok"),
        P("grp", "tok"),
        P("grp", None),
        P(None, "tok", ("fac", "sub")),
        P(None, "tok", ("fac", "sub")),
        P(None, ("fac", "sub")),
        P(None, ("fac", "sub")),
    )
    return jax.shard_map(
        body, mesh=mesh, in_specs=placed, out_specs=P("fac", ("grp", "tok", "sub")), check_vma=False
    )
```

profile of v0, /device:TPU:0, one launch (start us, length us, event | category | flops | bytes accessed | tf_op | source)
XLA Modules:
  0.0 804.6 jit_solution(17705837061198928718)
XLA Ops:
  6.5 2.6 copy.46
  9.2 6.3 all-to-all-start.1
  19.8 27.2 %all-to-all-done.1 = bf16[128,4,1280]{2,0,1:T(8,128)(2,1)} async-done(((bf16[128,4,1280]{2,0,1:T(8,128)(2,1)}), bf16[128,4,1280]{2,0,1:T(8,128)(2,1)}, u32[]{:S(2)}, u32[]{:S(2)}) %all-to-all-start.1) | async-done | bytes 1310752 | tf_op jit(solution)/shard_map/all_to_all | solution.py:56
  47.0 1.9 fusion.11
  49.0 6.9 convolution_multiply_fusion.1
  57.7 2.3 reduce-window.16
  60.7 1.5 reduce-window.19
  66.2 1.9 fusion.12
  68.2 3.4 fusion.7
  71.5 6.9 fusion.4
  78.4 27.4 %fusion = f32[2,2,160,3456]{3,2,1,0:T(8,128)} fusion(bf16[2,3456,3456]{2,1,0:T(8,128)(2,1)} %param.17, bf16[2,2,160,3456]{3,2,0,1:T(8,128)(2,1)} %fusion.7), kind=kOutput, calls=%fused_computation | convolution fusion | flops 15288238080 | bytes 61046784 | tf_op jit(solution)/shard_map/cfqr,crk->cfqk/dot_general | solution.py:90
  105.8 2.0 copy-done.2
  107.8 2.0 copy.45
  109.8 3.7 all-to-all-start
  113.8 1.4 add_divide_fusion
  115.2 155.8 %all-to-all-done = bf16[128,4,3456]{2,0,1:T(8,128)(2,1)S(1)} async-done(((bf16[128,4,3456]{2,0,1:T(8,128)(2,1)}), bf16[128,4,3456]{2,0,1:T(8,128)(2,1)S(1)}, u32[]{:S(2)}, u32[]{:S(2)}) %all-to-all-start) | async-done | bytes 3538976 | tf_op jit(solution)/shard_map/all_to_all | solution.py:55
  272.2 2.5 copy.18
  274.7 27.6 %convolution_multiply_fusion = f32[2,320,3456]{2,1,0:T(8,128)} fusion(bf16[2,320,3456]{2,1,0:T(8,128)(2,1)} %bitcast.117, bf16[2,3456,3456]{2,1,0:T(8,128)(2,1)} %param.17, f32[2,3456]{1,0:T(2,128)S(1)} %copy-done.4), kind=kOutput, calls=%fused_computation.8 | convolution fusion | flops 15290449920 | bytes 61074432 | tf_op jit(solution)/shard_map/csr,crk->csk/dot_general | solution.py:66
  305.1 291.2 %all-reduce.3.cloned.1.call-done = (f32[2,2,160,3456]{3,2,1,0:T(8,128)}, f32[2,2,160,1280]{3,2,1,0:T(8,128)}) async-done(((f32[2,2,160,3456]{3,2,1,0:T(8,128)}, f32[2,2,160,1280]{3,2,1,0:T(8,128)}), (f32[2,2,160,3456]{3,2,1,0:T(8,128)}, f32[2,2,160,1280]{3,2,1,0:T(8,128)})) %all-reduce.3.cloned.1.call-update) | async-done | bytes 12124176 | tf_op jit(solution)/shard_map/psum | solution.py:92
  596.2 5.6 fusion.17
  602.9 146.4 %reduce-scatter.5.cloned.1.call-done = f32[2,80,3456]{2,1,0:T(8,128)} async-done(((f32[2,320,3456]{2,1,0:T(8,128)}), f32[2,80,3456]{2,1,0:T(8,128)}) %reduce-scatter.5.cloned.1.call-update) | async-done | bytes 2211856 | tf_op jit(solution)/shard_map/reduce_scatter | solution.py:94
  749.3 12.3 %fusion.14 = f32[2,2,2,160,40]{3,4,0,1,2:T(8,128)S(1)} fusion(f32[2,2,40,3456,1]{3,2,4,1,0:T(8,128)} %bitcast.119, f32[2,2,160,3456]{3,2,1,0:T(8,128)} %get-tuple-element.5), kind=kOutput, calls=%fused_computation.22 | convolution fusion | flops 2123366400 | bytes 11264000 | tf_op jit(solution)/shard_map/cfqk,cspk->fscqp/dot_general | solution.py:99
  763.0 10.2 %reduce-scatter.11.cloned.1.call-done = f32[1,2,160,40]{2,3,1,0:T(8,128)} async-done(((f32[4,2,160,40]{2,3,1,0:T(8,128)}), f32[1,2,160,40]{2,3,1,0:T(8,128)}) %reduce-scatter.11.cloned.1.call-update) | async-done | bytes 51216 | tf_op jit(solution)/shard_map/reduce_scatter | solution.py:105
  773.2 22.8 %reduce-scatter.7.cloned.1.call-done = f32[1,2,160,40]{2,3,1,0:T(8,128)} async-done(((f32[4,2,160,40]{2,3,1,0:T(8,128)}), f32[1,2,160,40]{2,3,1,0:T(8,128)}) %reduce-scatter.7.cloned.1.call-update) | async-done | bytes 51216 | tf_op jit(solution)/shard_map/reduce_scatter | solution.py:104
  (60 shorter events, 19.7 us)
Async XLA Ops:
  6.5 61.6 %copy-start = (bf16[512,3456]{1,0:T(8,128)(2,1)S(1)}, bf16[512,3456]{1,0:T(8,128)(2,1)}, u32[]{:S(2)}) copy-start(bf16[512,3456]{1,0:T(8,128)(2,1)} %param.14) | copy-start | bytes 10616836
  6.5 9.5 %copy-start.7 = (s32[512,1]{0,1:T(1,128)S(1)}, s32[512,1]{0,1:T(1,128)}, u32[]{:S(2)}) copy-start(s32[512,1]{0,1:T(1,128)} %param.12) | copy-start | bytes 6148
  9.2 37.8 %all-to-all-start.1 = ((bf16[128,4,1280]{2,0,1:T(8,128)(2,1)}), bf16[128,4,1280]{2,0,1:T(8,128)(2,1)}, u32[]{:S(2)}, u32[]{:S(2)}) async-start(bf16[128,4,1280]{2,0,1:T(8,128)(2,1)} %bitcast.116), calls=%async_computation.3 | async-start | bytes 2621440 | tf_op jit(solution)/shard_map/all_to_all | solution.py:56
  15.5 289.6 %reduce-scatter.9.cloned.1.call-start = ((), (), s32[]{:S(2)}) async-start(), calls=%async_computation.8 | async-start | bytes 4096000 | tf_op jit(solution)/shard_map/reduce_scatter | solution.py:95
  47.0 2.0 copy-start.3
  49.0 6.9 copy-start.5
  55.9 540.4 %all-reduce.3.cloned.1.call-start = ((), (), s32[]{:S(2)}) async-start(), calls=%async_computation.10 | async-start | bytes 24248320 | tf_op jit(solution)/shard_map/psum | solution.py:92
  105.8 2.0 copy-start.2
  109.8 161.1 %all-to-all-start = ((bf16[128,4,3456]{2,0,1:T(8,128)(2,1)}), bf16[128,4,3456]{2,0,1:T(8,128)(2,1)S(1)}, u32[]{:S(2)}, u32[]{:S(2)}) async-start(bf16[128,4,3456]{2,0,1:T(8,128)(2,1)} %bitcast.115), calls=%async_computation | async-start | bytes 7077888 | tf_op jit(solution)/shard_map/all_to_all | solution.py:55
  113.6 635.8 %reduce-scatter.5.cloned.1.call-start = ((), (), s32[]{:S(2)}) async-start(), calls=%async_computation.6 | async-start | bytes 11059200 | tf_op jit(solution)/shard_map/reduce_scatter | solution.py:94
  272.2 2.5 copy-start.4
  302.3 0.7 copy-start.6
  302.3 470.9 %reduce-scatter.11.cloned.1.call-start = ((), (), s32[]{:S(2)}) async-start(), calls=%async_computation.9 | async-start | bytes 409600 | tf_op jit(solution)/shard_map/reduce_scatter | solution.py:105
  602.7 193.4 %reduce-scatter.7.cloned.1.call-start = ((), (), s32[]{:S(2)}) async-start(), calls=%async_computation.7 | async-start | bytes 409600 | tf_op jit(solution)/shard_map/reduce_scatter | solution.py:104
  749.3 48.8 %copy-start.1 = (bf16[512,3456]{1,0:T(8,128)(2,1)S(1)}, bf16[512,3456]{1,0:T(8,128)(2,1)}, u32[]{:S(2)}) copy-start(bf16[512,3456]{1,0:T(8,128)(2,1)} %param.14) | copy-start | bytes 10616836
Sparse Core Ops, SparseCore 0:
  56.0 61.4 reduce-scatter.8
  120.1 476.1 all-reduce.2
  598.6 150.6 reduce-scatter.4
  751.8 21.3 reduce-scatter.10
  775.5 20.4 reduce-scatter.6
where the time goes:
time: 806 us; the launch traced here: 805 us
  waiting for transfers between devices  654 us (81%)
  matrix products  97.1 us (12%)
  local copies, waits for them, and re-layouts  16.3 us (2%)
  other arithmetic  13.6 us (2%)
  between operations  13.3 us (2%)
  starting transfers between devices  10.6 us (1%)
    psum x1, waiting for transfers between devices, body(): query_g, query_a = lax.psum((partial_g, partial_a), 'tok')  291 us
    all_to_all x1, waiting for transfers between devices, body(): lax.all_to_all(gradients, 'tok', split_axis=1, concat_axis=0, tiled=True)  156 us
    reduce_scatter x1, waiting for transfers between devices, body(): lax.psum_scatter(coords_g, 'tok', scatter_dimension=1, tiled=True)  146 us
    dot_general x1, matrix products, body(): jnp.einsum('csr,crk->csk', moved_g, basis_g, preferred_element_type=jnp.f...  27.6 us
    dot_general x1, matrix products, body(): jnp.einsum('cfqr,crk->cfqk', qpacked_g, basis_g, preferred_element_type=j...  27.4 us
    all_to_all x1, waiting for transfers between devices, body(): lax.all_to_all(activations, 'tok', split_axis=1, concat_axis=0, tiled=True)  27.2 us
    reduce_scatter x1, waiting for transfers between devices, body(): lax.psum_scatter(pieces_g, ('fac', 'sub'), scatter_dimension=0, tiled=True)  22.8 us
  transfers between devices with their start and end apart: 7, of which 6 were waited for; matrix products, arithmetic and copies ran while one was open for 14% of the time, Pallas kernels for 0%

commit v1 on v0

v1 whole, which is shorter than its diff:
```python
import math

import jax
import jax.numpy as jnp
from jax import lax
from jax.sharding import PartitionSpec as P

D = 5120
FH = 13824
DAMPING = 0.25
CHUNKS = 8
LARGEST = 32767.0


def quantise(x):
    top = jnp.max(jnp.abs(x), axis=1, keepdims=True)
    code = jnp.ceil(8.0 * jnp.log2(jnp.maximum(top, 1e-30)))
    scaled = jnp.round(x * (LARGEST * jnp.exp2(code * -0.125)))
    return jnp.clip(scaled, -LARGEST, LARGEST).astype(jnp.int16), code.astype(jnp.int16)


def pack(x_g, x_a):
    q_g, e_g = quantise(x_g)
    q_a, e_a = quantise(x_a)
    lane = lax.broadcasted_iota(jnp.int32, (x_g.shape[0], 128), 1)
    tail = jnp.where(lane < 64, e_g, e_a)
    return jnp.concatenate([q_g, q_a, tail], axis=1)


def unpack(packet, width_g, width_a):
    both = width_g + width_a
    s_g = jnp.exp2(packet[:, both : both + 1].astype(jnp.float32) * 0.125) * (1.0 / LARGEST)
    s_a = jnp.exp2(packet[:, both + 64 : both + 65].astype(jnp.float32) * 0.125) * (1.0 / LARGEST)
    return (
        packet[:, :width_g].astype(jnp.float32) * s_g,
        packet[:, width_g:both].astype(jnp.float32) * s_a,
    )


def body(
    activations,
    gradients,
    tok_class,
    query_inputs,
    query_gradients,
    query_class,
    basis_a,
    basis_g,
    eigen_a,
    eigen_g,
):
    classes, width_g, width_a = basis_g.shape[0], basis_g.shape[2], basis_a.shape[2]
    deep_g, deep_a = basis_g.shape[1], basis_a.shape[1]
    tok_count, fac_count, sub_count = (lax.axis_size(a) for a in ("tok", "fac", "sub"))
    z, x, core = (lax.axis_index(a) for a in ("tok", "fac", "sub"))
    queries = query_inputs.shape[0]
    block = queries // fac_count
    rows = block // CHUNKS
    low, high = 3 * CHUNKS // 8, 5 * CHUNKS // 8
    tok_rows = activations.shape[0]
    half_rows = tok_rows // sub_count
    slot_cap = 5 * half_rows // 8
    share = half_rows // fac_count
    token_ids = tok_class[:, 0]
    query_ids = query_class[:, 0]

    at = (core * fac_count + x) * share
    own_g = lax.dynamic_slice_in_dim(gradients, at, share)
    own_a = lax.dynamic_slice_in_dim(activations, at, share)
    blocks = []
    for step in range(tok_count):
        to = lax.rem(z + step, tok_count)
        part = jnp.concatenate(
            [
                lax.dynamic_slice_in_dim(own_g, to * deep_g, deep_g, 1),
                lax.dynamic_slice_in_dim(own_a, to * deep_a, deep_a, 1),
            ],
            axis=1,
        )
        if step:
            part = lax.ppermute(part, "tok", [(i, (i + step) % tok_count) for i in range(tok_count)])
        blocks.append(part)
    mine = jnp.concatenate(blocks, axis=0)
    plane = [mine]
    for step in range(1, fac_count):
        plane.append(lax.ppermute(mine, "fac", [(i, (i + step) % fac_count) for i in range(fac_count)]))
    plane = jnp.concatenate(plane, axis=0)
    other = [plane]
    for step in range(1, sub_count):
        other.append(lax.ppermute(plane, "sub", [(i, (i + step) % sub_count) for i in range(sub_count)]))
    raw = jnp.concatenate(other, axis=0)

    halves = tok_count * sub_count
    ids = token_ids.reshape(halves, half_rows)
    earlier = jnp.arange(half_rows)[None, :] < jnp.arange(half_rows)[:, None]
    rank = jnp.sum(
        ((ids[:, None, :] == ids[:, :, None]) & earlier).astype(jnp.int32), axis=2
    )
    slot = ids * (halves * slot_cap) + jnp.arange(halves)[:, None] * slot_cap + rank
    from_s = lax.rem(core - jnp.arange(sub_count) + sub_count, sub_count)[:, None, None, None]
    from_f = lax.rem(x - jnp.arange(fac_count) + fac_count, fac_count)[None, :, None, None]
    from_z = lax.rem(z - jnp.arange(tok_count) + tok_count, tok_count)[None, None, :, None]
    slot = slot.reshape(tok_count, sub_count, fac_count, share)
    pick_s = from_s[:, 0, 0, 0]
    slot = jnp.take(jnp.take(jnp.take(slot, from_z[0, 0, :, 0], 0), pick_s, 1), from_f[0, :, 0, 0], 2)
    slot = slot.transpose(1, 2, 0, 3).reshape(-1)
    table = (jnp.arange(classes * halves * slot_cap)[:, None] == slot[None, :]).astype(jnp.bfloat16)
    packed = jnp.dot(table, raw, preferred_element_type=jnp.float32).astype(jnp.bfloat16)
    packed = packed.reshape(classes, halves * slot_cap, deep_g + deep_a)

    qids = query_ids.reshape(fac_count, block)
    key = qids * block + jnp.arange(block)
    place = jnp.sum((key[:, None, :] < key[:, :, None]).astype(jnp.int32), axis=2)
    first = jnp.sum((qids == 0).astype(jnp.int32), axis=1)
    order = (jnp.arange(block)[None, :, None] == place[:, None, :]).astype(jnp.bfloat16)
    order = order.reshape(fac_count, CHUNKS, rows, block)

    def ordered(features):
        return (
            jnp.einsum(
                "fjpb,fbr->jfpr",
                order,
                features.reshape(fac_count, block, features.shape[1]),
                preferred_element_type=jnp.float32,
            )
            .astype(jnp.bfloat16)
            .reshape(queries, features.shape[1])
        )

    unit = fac_count * rows
    spot = (jnp.arange(low, high)[:, None, None] * rows + jnp.arange(rows)) < first[None, :, None]
    spot = spot.reshape((high - low) * unit, 1)

    def partial(features, basis):
        sorted_rows = ordered(features)
        zero = jnp.dot(sorted_rows[: high * unit], basis[0], preferred_element_type=jnp.float32)
        one = jnp.dot(sorted_rows[low * unit :], basis[1], preferred_element_type=jnp.float32)
        middle = jnp.where(spot, zero[low * unit :], one[: (high - low) * unit])
        out = jnp.concatenate([zero[: low * unit], middle, one[(high - low) * unit :]], axis=0)
        return out.reshape(CHUNKS, unit, basis.shape[2])

    part_a = partial(query_inputs, basis_a)
    part_g = partial(query_gradients, basis_g)

    weight_g = 1.0 / (eigen_g + DAMPING)
    weight_a = 1.0 / (eigen_a + DAMPING)
    tok_g = (
        jnp.einsum("csr,crk->csk", packed[:, :, :deep_g], basis_g, preferred_element_type=jnp.float32)
        * weight_g[:, None, :]
    )
    tok_a = (
        jnp.einsum("csr,crk->csk", packed[:, :, deep_g:], basis_a, preferred_element_type=jnp.float32)
        * weight_a[:, None, :]
    )

    up = [(i, i + 1) for i in range(tok_count - 1)]
    down = [(i + 1, i) for i in range(tok_count - 1)]
    from_below, from_above = [], []
    for step in range(CHUNKS + tok_count - 2):
        for got, pairs, behind in (
            (from_below, up, z),
            (from_above, down, tok_count - 1 - z),
        ):
            chunk = jnp.clip(step - behind, 0, CHUNKS - 1)
            x_g = lax.dynamic_index_in_dim(part_g, chunk, 0, keepdims=False)
            x_a = lax.dynamic_index_in_dim(part_a, chunk, 0, keepdims=False)
            if step:
                r_g, r_a = unpack(got[-1], width_g, width_a)
                x_g, x_a = x_g + r_g, x_a + r_a
            got.append(lax.ppermute(pack(x_g, x_a), "tok", pairs))

    sides = {0: [], 1: []}
    for chunk in range(CHUNKS):
        below = jnp.zeros_like(from_below[0])
        above = jnp.zeros_like(from_above[0])
        for behind in range(1, tok_count):
            below = jnp.where(z == behind, from_below[chunk + behind - 1], below)
            above = jnp.where(tok_count - 1 - z == behind, from_above[chunk + behind - 1], above)
        b_g, b_a = unpack(below, width_g, width_a)
        a_g, a_a = unpack(above, width_g, width_a)
        full_g = part_g[chunk] + b_g + a_g
        full_a = part_a[chunk] + b_a + a_a
        for klass in range(classes):
            if (chunk < high, chunk >= low)[klass]:
                s_g = lax.dot_general(
                    full_g, tok_g[klass], (((1,), (1,)), ((), ())), precision=lax.Precision.HIGH,
                    preferred_element_type=jnp.float32,
                )
                s_a = lax.dot_general(
                    full_a, tok_a[klass], (((1,), (1,)), ((), ())), precision=lax.Precision.HIGH,
                    preferred_element_type=jnp.float32,
                )
                sides[klass].append(jnp.stack([s_g, s_a]).reshape(2, fac_count, rows, halves, slot_cap))
    pieces = jnp.stack([jnp.concatenate(sides[k], axis=2) for k in range(classes)])
    pieces = pieces.transpose(4, 2, 0, 1, 3, 5).reshape(
        tok_count, sub_count, fac_count, classes, 2, high * rows, slot_cap
    )
    pieces = pieces.transpose(0, 2, 1, 3, 4, 5, 6).reshape(
        tok_count * fac_count * sub_count, classes, 2, high * rows, slot_cap
    )
    side = lax.psum_scatter(pieces, ("tok", "fac", "sub"), scatter_dimension=0, tiled=True)[0]
    scores = side[:, 0] * side[:, 1] * (1.0 / math.sqrt(FH * D))

    own_place = lax.dynamic_index_in_dim(place, x, 0, keepdims=False)
    own_first = lax.dynamic_index_in_dim(first, x, 0, keepdims=False)
    at_row = jnp.arange(high * rows)
    out = jnp.zeros((block, half_rows), jnp.float32)
    half = z * sub_count + core
    own_rank = lax.dynamic_index_in_dim(rank, half, 0, keepdims=False)
    own_ids = lax.dynamic_index_in_dim(ids, half, 0, keepdims=False)
    for klass in range(classes):
        row = at_row + (0, low * rows)[klass]
        of_class = (row < own_first) if klass == 0 else (row >= own_first)
        to_query = ((own_place[:, None] == row[None, :]) & of_class[None, :]).astype(jnp.float32)
        to_token = (
            (own_rank[None, :] == jnp.arange(slot_cap)[:, None]) & (own_ids[None, :] == klass)
        ).astype(jnp.float32)
        by_query = jnp.dot(to_query, scores[klass], precision=lax.Precision.HIGHEST)
        out = out + jnp.dot(by_query, to_token, precision=lax.Precision.HIGHEST)
    return out


def solution(mesh):
    placed = (
        P(("grp", "tok"), None),
        P(("grp", "tok"), None),
        P("grp", None),
        P("grp", "tok"),
        P("grp", "tok"),
        P("grp", None),
        P(None, "tok", ("fac", "sub")),
        P(None, "tok", ("fac", "sub")),
        P(None, ("fac", "sub")),
        P(None, ("fac", "sub")),
    )
    return jax.shard_map(
        body, mesh=mesh, in_specs=placed, out_specs=P("fac", ("grp", "tok", "sub")), check_vma=False
    )
```

time: 806 us -> 728 us (0.903); the launches traced: 805 us -> 718 us
  waiting for transfers between devices: 654 us -> 107 us
  other arithmetic: 13.6 us -> 183 us
  local copies, waits for them, and re-layouts: 16.3 us -> 180 us
  matrix products: 97.1 us -> 164 us
  starting transfers between devices: 10.6 us -> 69.9 us
    psum x1 -> x0, waiting for transfers between devices: 291 us -> none  [body(): query_g, query_a = lax.psum((partial_g, partial_a), 'tok')]
    all_to_all x2 -> x0, waiting for transfers between devices: 183 us -> none  [the longest x1 156 us: body(): lax.all_to_all(gradients, 'tok', split_axis=1, concat_axis=0, tiled=True)]
    reduce_scatter x4 -> x1, waiting for transfers between devices: 179 us -> 59.4 us  [body(): lax.psum_scatter(pieces, ('tok', 'fac', 'sub'), scatter_dimension=0, tile...]
    ppermute x0 -> x25, starting transfers between devices: none -> 69.9 us  [the longest x20 60.5 us: body(): got.append(lax.ppermute(pack(x_g, x_a), 'tok', pairs))]
    dot_general x12 -> x33, matrix products: 97.1 us -> 164 us  [the longest x10 61.4 us: body(): lax.dot_general(full_g, tok_g[klass], (((1,), (1,)), ((), ())), precision...]
    ppermute x0 -> x25, waiting for transfers between devices: none -> 47.8 us  [the longest x20 47.8 us: body(): got.append(lax.ppermute(pack(x_g, x_a), 'tok', pairs))]
    unnamed x18 -> x156, local copies, waits for them, and re-layouts: 3.13 us -> 49.3 us
    add x0 -> x18, other arithmetic: none -> 44.8 us  [the longest x7 26.4 us: body(): full_g = part_g[chunk] + b_g + a_g]
  transfers between devices with their start and end apart: 7 -> 26, of which waited for: 6 -> 9; matrix products, arithmetic and copies ran while one was open for 14% -> 37% of each run, Pallas kernels for 0% -> 0%
where the time goes in v1:
time: 728 us; the launch traced here: 718 us
  other arithmetic  183 us (25%)
  local copies, waits for them, and re-layouts  180 us (25%)
  matrix products  164 us (23%)
  waiting for transfers between devices  107 us (15%)
  starting transfers between devices  69.9 us (10%)
  between operations  15.4 us (2%)
    dot_general x10, matrix products, body(): lax.dot_general(full_g, tok_g[klass], (((1,), (1,)), ((), ())), precision...  61.4 us
    ppermute x20, starting transfers between devices, body(): got.append(lax.ppermute(pack(x_g, x_a), 'tok', pairs))  60.5 us
    reduce_scatter x1, waiting for transfers between devices, body(): lax.psum_scatter(pieces, ('tok', 'fac', 'sub'), scatter_dimension=0, tile...  59.4 us
    unnamed x156, local copies, waits for them, and re-layouts  49.3 us
    ppermute x20, waiting for transfers between devices, body(): got.append(lax.ppermute(pack(x_g, x_a), 'tok', pairs))  47.8 us
    ppermute x20, local copies, waits for them, and re-layouts, body(): got.append(lax.ppermute(pack(x_g, x_a), 'tok', pairs))  42.9 us
    reduce_max x23, other arithmetic, quantise(): top = jnp.max(jnp.abs(x), axis=1, keepdims=True)  31.8 us
    convert_element_type x23, other arithmetic, quantise(): jnp.clip(scaled, -LARGEST, LARGEST).astype(jnp.int16)  30.9 us
  transfers between devices with their start and end apart: 26, of which 9 were waited for; matrix products, arithmetic and copies ran while one was open for 37% of the time, Pallas kernels for 0%

profile of v1, /device:TPU:0, one launch (start us, length us, event | category | flops | bytes accessed | tf_op | source)
XLA Modules:
  0.0 718.4 jit_solution(9090297222561135530)
XLA Ops:
  37.6 13.2 %fusion = f32[320,3456]{1,0:T(8,128)S(1)} fusion(bf16[320,3456]{1,0:T(8,128)(2,1)S(1)} %bitcast.737, bf16[2,3456,3456]{2,1,0:T(8,128)(2,1)} %param.17), kind=kOutput, calls=%fused_computation.3 | convolution fusion | flops 7644119040 | bytes 30523392 | tf_op jit(solution)/shard_map/dot_general | solution.py:137
  54.3 13.0 %fusion.2 = f32[320,3456]{1,0:T(8,128)S(1)} fusion(bf16[320,3456]{1,0:T(8,128)(2,1)S(1)} %bitcast.738, bf16[2,3456,3456]{2,1,0:T(8,128)(2,1)} %param.17), kind=kOutput, calls=%fused_computation.5 | convolution fusion | flops 7644119040 | bytes 30523392 | tf_op jit(solution)/shard_map/dot_general | solution.py:136
  163.9 8.6 %collective-permute-done.3 = s16[64,4864]{1,0:T(8,128)(2,1)S(1)} collective-permute-done((s16[64,4864]{1,0:T(8,128)(2,1)S(1)}, s16[64,4864]{1,0:T(8,128)(2,1)S(1)}, u32[]{:S(2)}, u32[]{:S(2)}) %collective-permute-start.3) | collective-permute-done | bytes 622624 | tf_op jit(solution)/shard_map/ppermute | solution.py:170
  181.6 11.6 %collective-permute-done.4 = s16[64,4864]{1,0:T(8,128)(2,1)S(1)} collective-permute-done((s16[64,4864]{1,0:T(8,128)(2,1)S(1)}, s16[64,4864]{1,0:T(8,128)(2,1)S(1)}, u32[]{:S(2)}, u32[]{:S(2)}) %collective-permute-start.4) | collective-permute-done | bytes 622624 | tf_op jit(solution)/shard_map/ppermute | solution.py:170
  203.1 5.4 collective-permute-start.2
  237.3 7.9 %collective-permute-done.12 = s16[64,4864]{1,0:T(8,128)(2,1)} collective-permute-done((s16[64,4864]{1,0:T(8,128)(2,1)S(1)}, s16[64,4864]{1,0:T(8,128)(2,1)}, u32[]{:S(2)}, u32[]{:S(2)}) %collective-permute-start.12) | collective-permute-done | bytes 622624 | tf_op jit(solution)/shard_map/ppermute | solution.py:170
  266.5 7.6 %collective-permute-done.14 = s16[64,4864]{1,0:T(8,128)(2,1)} collective-permute-done((s16[64,4864]{1,0:T(8,128)(2,1)S(1)}, s16[64,4864]{1,0:T(8,128)(2,1)}, u32[]{:S(2)}, u32[]{:S(2)}) %collective-permute-start.14) | collective-permute-done | bytes 622624 | tf_op jit(solution)/shard_map/ppermute | solution.py:170
  288.9 5.4 collective-permute-start.15
  294.3 7.6 %convolution_convert_fusion = bf16[640,4736]{1,0:T(8,128)(2,1)} fusion(bf16[512,4736]{1,0:T(8,128)(2,1)} %constant_dynamic-update-slice_fusion.4, s32[512]{0:T(512)S(1)} %eq.101), kind=kOutput, calls=%fused_computation.9 | convolution fusion | flops 3107143680 | bytes 10913792 | tf_op jit(solution)/shard_map/dot_general | solution.py:108
  317.4 5.6 collective-permute-start.17
  322.9 27.2 %convolution_multiply_fusion = f32[2,320,3456]{2,1,0:T(8,128)} fusion(bf16[2,3456,3456]{2,1,0:T(8,128)(2,1)} %param.17, bf16[2,320,4736]{2,1,0:T(8,128)(2,1)} %bitcast.753, f32[2,3456]{1,0:T(2,128)S(1)} %add_divide_fusion), kind=kOutput, calls=%fused_computation.11 | convolution fusion | flops 15290449920 | bytes 61074432 | tf_op jit(solution)/shard_map/csr,crk->csk/dot_general | solution.py:148
  365.6 5.4 collective-permute-start.19
  392.7 6.2 collective-permute-start.21
  398.8 7.4 %convolution_multiply_fusion.1 = f32[2,320,1280]{2,1,0:T(8,128)} fusion(bf16[2,1280,1280]{2,1,0:T(8,128)(2,1)} %param.16, bf16[2,320,4736]{2,1,0:T(8,128)(2,1)} %bitcast.754, f32[2,1280]{1,0:T(2,128)S(1)} %add_divide_fusion.1), kind=kOutput, calls=%fused_computation.16 | convolution fusion | flops 2097971200 | bytes 11479040 | tf_op jit(solution)/shard_map/csr,crk->csk/dot_general | solution.py:152
  421.5 5.4 collective-permute-start.23
  433.9 8.1 %select_select_fusion.10 = (s16[64,4864]{0,1:T(8,128)(2,1)}, s16[64,4864]{0,1:T(8,128)(2,1)}, s16[64,4864]{0,1:T(8,128)(2,1)}, s16[64,4864]{0,1:T(8,128)(2,1)S(1...) fusion(s16[64,4864]{0,1:T(8,128)(2,1)} %copy.258, ...), kind=kLoop, calls=%fused_computation.48 | loop fusion | flops 7471104 | bytes 11206659 | tf_op jit(solution)/shard_map/jit(_where)/select_n | solution.py:178
  446.1 8.4 %select_select_fusion.11 = (s16[64,4864]{0,1:T(8,128)(2,1)}, s16[64,4864]{0,1:T(8,128)(2,1)}, s16[64,4864]{0,1:T(8,128)(2,1)}, s16[64,4864]{0,1:T(8,128)(2,1)S(1...) fusion(s16[64,4864]{0,1:T(8,128)(2,1)} %copy.253, ...), kind=kLoop, calls=%fused_computation.49 | loop fusion | flops 7471104 | bytes 11206659 | tf_op jit(solution)/shard_map/jit(_where)/select_n | solution.py:177
  481.3 8.2 %convolution_bitcast_fusion.7 = f32[1,2,32,8,40]{4,2,3,1,0:T(8,128)} fusion(f32[2,32,3456,1]{2,1,3,0:T(8,128)} %bitcast.721, f32[8,40,3456,1]{2,1,0,3:T(8,128)} %bitcast.671), kind=kOutput, calls=%fused_computation.62 | convolution fusion | flops 424673280 | bytes 5390336 | tf_op jit(solution)/shard_map/dot_general | solution.py:185
  489.5 8.0 %convolution_bitcast_fusion.9 = f32[1,2,32,8,40]{4,2,3,1,0:T(8,128)} fusion(f32[2,32,3456,1]{2,1,3,0:T(8,128)S(1)} %bitcast.723, f32[8,40,3456,1]{2,1,0,3:T(8,128)} %bitcast.672), kind=kOutput, calls=%fused_computation.64 | convolution fusion | flops 424673280 | bytes 5390336 | tf_op jit(solution)/shard_map/dot_general | solution.py:185
  497.5 7.9 %convolution_bitcast_fusion.13 = f32[1,2,32,8,40]{4,2,3,1,0:T(8,128)} fusion(f32[2,32,3456,1]{2,1,3,0:T(8,128)S(1)} %bitcast.724, f32[8,40,3456,1]{2,1,0,3:T(8,128)} %bitcast.678), kind=kOutput, calls=%fused_computation.68 | convolution fusion | flops 424673280 | bytes 5390336 | tf_op jit(solution)/shard_map/dot_general | solution.py:185
  505.4 5.6 convolution_bitcast_fusion.11
  599.0 6.8 convolution_bitcast_fusion.15
  636.2 5.8 copy.328
  647.8 59.4 %reduce-scatter.2.cloned.1.call-done = f32[1,2,2,160,40]{3,4,2,1,0:T(8,128)} async-done(((f32[16,2,2,160,40]{3,4,2,1,0:T(8,128)}), f32[1,2,2,160,40]{3,4,2,1,0:T(8,128)}) %reduce-scatter.2.cloned.1.call-update) | async-done | bytes 102416 | tf_op jit(solution)/shard_map/reduce_scatter | solution.py:201
  (520 shorter events, 447.5 us)
Async XLA Ops:
  6.5 700.7 %reduce-scatter.2.cloned.1.call-start = ((), (), s32[]{:S(2)}) async-start(), calls=%async_computation.1 | async-start | bytes 2785280 | tf_op jit(solution)/shard_map/reduce_scatter | solution.py:201
  11.6 146.6 %collective-permute-start.7 = (bf16[32,4736]{1,0:T(8,128)(2,1)}, bf16[32,4736]{1,0:T(8,128)(2,1)}, u32[]{:S(2)}, u32[]{:S(2)}) collective-permute-start(bf16[32,4736]{1,0:T(8,128)(2,1)} %pad_maximum_fusion.5), channel_id=1, source_target_pairs={{0,8},{4,12},{8,0},{12,4},{1,9},{5,13},{9,1},{13,5},{2,10},{6,14},... | collective-permute-start | bytes 909320 | tf_op jit(solution)/shard_map/ppermute | solution.py:81
  16.3 141.8 %collective-permute-start.6 = (bf16[32,4736]{1,0:T(8,128)(2,1)}, bf16[32,4736]{1,0:T(8,128)(2,1)}, u32[]{:S(2)}, u32[]{:S(2)}) collective-permute-start(bf16[32,4736]{1,0:T(8,128)(2,1)} %pad_maximum_fusion.4), channel_id=1, source_target_pairs={{0,4},{4,8},{8,12},{12,0},{1,5},{5,9},{9,13},{13,1},{2,6},{6,10},{... | collective-permute-start | bytes 909320 | tf_op jit(solution)/shard_map/ppermute | solution.py:81
  18.7 139.5 %collective-permute-start.8 = (bf16[32,4736]{1,0:T(8,128)(2,1)}, bf16[32,4736]{1,0:T(8,128)(2,1)}, u32[]{:S(2)}, u32[]{:S(2)}) collective-permute-start(bf16[32,4736]{1,0:T(8,128)(2,1)} %pad_maximum_fusion.6), channel_id=1, source_target_pairs={{0,12},{4,0},{8,4},{12,8},{1,13},{5,1},{9,5},{13,9},{2,14},{6,2},{... | collective-permute-start | bytes 909320 | tf_op jit(solution)/shard_map/ppermute | solution.py:81
  92.4 14.6 %collective-permute-start = (s16[64,4864]{1,0:T(8,128)(2,1)}, s16[64,4864]{1,0:T(8,128)(2,1)S(1)}, u32[]{:S(2)}, u32[]{:S(2)}) collective-permute-start(s16[64,4864]{1,0:T(8,128)(2,1)} %pad_add_fusion), channel_id=1, source_target_pairs={{0,4},{4,8},{8,12},{1,5},{5,9},{9,13},{2,6},{6,10},{10,14},{3,7},{... | collective-permute-start | bytes 1867784 | tf_op jit(solution)/shard_map/ppermute | solution.py:170
  114.5 36.5 %collective-permute-start.1 = (s16[64,4864]{1,0:T(8,128)(2,1)}, s16[64,4864]{1,0:T(8,128)(2,1)S(1)}, u32[]{:S(2)}, u32[]{:S(2)}) collective-permute-start(s16[64,4864]{1,0:T(8,128)(2,1)} %pad_add_fusion.1), channel_id=1, source_target_pairs={{0,4},{4,8},{8,12},{1,5},{5,9},{9,13},{2,6},{6,10},{10,14},{3,7},{... | collective-permute-start | bytes 1867784 | tf_op jit(solution)/shard_map/ppermute | solution.py:170
  156.9 15.6 %collective-permute-start.3 = (s16[64,4864]{1,0:T(8,128)(2,1)S(1)}, s16[64,4864]{1,0:T(8,128)(2,1)S(1)}, u32[]{:S(2)}, u32[]{:S(2)}) collective-permute-start(s16[64,4864]{1,0:T(8,128)(2,1)S(1)} %pad_add_fusion.3), channel_id=1, source_target_pairs={{4,0},{8,4},{12,8},{5,1},{9,5},{13,9},{6,2},{10,6},{14,10},{7,3},{... | collective-permute-start | bytes 1867784 | tf_op jit(solution)/shard_map/ppermute | solution.py:170
  160.5 73.9 %collective-permute-start.9 = (bf16[128,4736]{1,0:T(8,128)(2,1)}, bf16[128,4736]{1,0:T(8,128)(2,1)}, u32[]{:S(2)}, u32[]{:S(2)}) collective-permute-start(bf16[128,4736]{1,0:T(8,128)(2,1)} %pad_maximum_fusion.3), channel_id=1, source_target_pairs={{0,2},{2,0},{1,3},{3,1},{4,6},{6,4},{5,7},{7,5},{8,10},{10,8},{9,1... | collective-permute-start | bytes 3637256 | tf_op jit(solution)/shard_map/ppermute | solution.py:86
  178.4 14.8 %collective-permute-start.4 = (s16[64,4864]{1,0:T(8,128)(2,1)S(1)}, s16[64,4864]{1,0:T(8,128)(2,1)S(1)}, u32[]{:S(2)}, u32[]{:S(2)}) collective-permute-start(s16[64,4864]{1,0:T(8,128)(2,1)S(1)} %pad_add_fusion.4), channel_id=1, source_target_pairs={{4,0},{8,4},{12,8},{5,1},{9,5},{13,9},{6,2},{10,6},{14,10},{7,3},{... | collective-permute-start | bytes 1867784 | tf_op jit(solution)/shard_map/ppermute | solution.py:170
  200.9 13.9 %collective-permute-start.5 = (s16[64,4864]{1,0:T(8,128)(2,1)S(1)}, s16[64,4864]{1,0:T(8,128)(2,1)S(1)}, u32[]{:S(2)}, u32[]{:S(2)}) collective-permute-start(s16[64,4864]{1,0:T(8,128)(2,1)S(1)} %pad_add_fusion.5), channel_id=1, source_target_pairs={{4,0},{8,4},{12,8},{5,1},{9,5},{13,9},{6,2},{10,6},{14,10},{7,3},{... | collective-permute-start | bytes 1867784 | tf_op jit(solution)/shard_map/ppermute | solution.py:170
  203.1 14.1 %collective-permute-start.2 = (s16[64,4864]{1,0:T(8,128)(2,1)}, s16[64,4864]{1,0:T(8,128)(2,1)}, u32[]{:S(2)}, u32[]{:S(2)}) collective-permute-start(s16[64,4864]{1,0:T(8,128)(2,1)} %pad_add_fusion.2), channel_id=1, source_target_pairs={{0,4},{4,8},{8,12},{1,5},{5,9},{9,13},{2,6},{6,10},{10,14},{3,7},{... | collective-permute-start | bytes 1867784 | tf_op jit(solution)/shard_map/ppermute | solution.py:170
  228.3 20.3 %collective-permute-start.11 = (s16[64,4864]{1,0:T(8,128)(2,1)}, s16[64,4864]{1,0:T(8,128)(2,1)S(1)}, u32[]{:S(2)}, u32[]{:S(2)}) collective-permute-start(s16[64,4864]{1,0:T(8,128)(2,1)} %pad_add_fusion.6), channel_id=1, source_target_pairs={{0,4},{4,8},{8,12},{1,5},{5,9},{9,13},{2,6},{6,10},{10,14},{3,7},{... | collective-permute-start | bytes 1867784 | tf_op jit(solution)/shard_map/ppermute | solution.py:170
  232.7 12.5 %collective-permute-start.12 = (s16[64,4864]{1,0:T(8,128)(2,1)S(1)}, s16[64,4864]{1,0:T(8,128)(2,1)}, u32[]{:S(2)}, u32[]{:S(2)}) collective-permute-start(s16[64,4864]{1,0:T(8,128)(2,1)S(1)} %pad_add_fusion.7), channel_id=1, source_target_pairs={{4,0},{8,4},{12,8},{5,1},{9,5},{13,9},{6,2},{10,6},{14,10},{7,3},{... | collective-permute-start | bytes 1867784 | tf_op jit(solution)/shard_map/ppermute | solution.py:170
  237.3 25.9 %collective-permute-start.10 = (bf16[256,4736]{1,0:T(8,128)(2,1)}, bf16[256,4736]{1,0:T(8,128)(2,1)}, u32[]{:S(2)}, u32[]{:S(2)}) collective-permute-start(bf16[256,4736]{1,0:T(8,128)(2,1)} %get-tuple-element.191), channel_id=1, source_target_pairs={{0,1},{1,0},{2,3},{3,2},{4,5},{5,4},{6,7},{7,6},{8,9},{9,8},{10,11... | collective-permute-start | bytes 7274504 | tf_op jit(solution)/shard_map/ppermute | solution.py:90
  258.6 18.9 %collective-permute-start.13 = (s16[64,4864]{1,0:T(8,128)(2,1)}, s16[64,4864]{1,0:T(8,128)(2,1)S(1)}, u32[]{:S(2)}, u32[]{:S(2)}) collective-permute-start(s16[64,4864]{1,0:T(8,128)(2,1)} %pad_add_fusion.8), channel_id=1, source_target_pairs={{0,4},{4,8},{8,12},{1,5},{5,9},{9,13},{2,6},{6,10},{10,14},{3,7},{... | collective-permute-start | bytes 1867784 | tf_op jit(solution)/shard_map/ppermute | solution.py:170
  287.6 17.7 %collective-permute-start.16 = (s16[64,4864]{1,0:T(8,128)(2,1)}, s16[64,4864]{1,0:T(8,128)(2,1)S(1)}, u32[]{:S(2)}, u32[]{:S(2)}) collective-permute-start(s16[64,4864]{1,0:T(8,128)(2,1)} %pad_add_fusion.11), channel_id=1, source_target_pairs={{4,0},{8,4},{12,8},{5,1},{9,5},{13,9},{6,2},{10,6},{14,10},{7,3},{... | collective-permute-start | bytes 1867784 | tf_op jit(solution)/shard_map/ppermute | solution.py:170
  288.9 13.0 %collective-permute-start.15 = (s16[64,4864]{1,0:T(8,128)(2,1)S(1)}, s16[64,4864]{1,0:T(8,128)(2,1)}, u32[]{:S(2)}, u32[]{:S(2)}) collective-permute-start(s16[64,4864]{1,0:T(8,128)(2,1)S(1)} %pad_add_fusion.10), channel_id=1, source_target_pairs={{0,4},{4,8},{8,12},{1,5},{5,9},{9,13},{2,6},{6,10},{10,14},{3,7},{... | collective-permute-start | bytes 1867784 | tf_op jit(solution)/shard_map/ppermute | solution.py:170
  315.2 38.3 %collective-permute-start.18 = (s16[64,4864]{1,0:T(8,128)(2,1)}, s16[64,4864]{1,0:T(8,128)(2,1)S(1)}, u32[]{:S(2)}, u32[]{:S(2)}) collective-permute-start(s16[64,4864]{1,0:T(8,128)(2,1)} %pad_add_fusion.13), channel_id=1, source_target_pairs={{4,0},{8,4},{12,8},{5,1},{9,5},{13,9},{6,2},{10,6},{14,10},{7,3},{... | collective-permute-start | bytes 1867784 | tf_op jit(solution)/shard_map/ppermute | solution.py:170
  317.4 32.8 %collective-permute-start.17 = (s16[64,4864]{1,0:T(8,128)(2,1)}, s16[64,4864]{1,0:T(8,128)(2,1)}, u32[]{:S(2)}, u32[]{:S(2)}) collective-permute-start(s16[64,4864]{1,0:T(8,128)(2,1)} %pad_add_fusion.12), channel_id=1, source_target_pairs={{0,4},{4,8},{8,12},{1,5},{5,9},{9,13},{2,6},{6,10},{10,14},{3,7},{... | collective-permute-start | bytes 1867784 | tf_op jit(solution)/shard_map/ppermute | solution.py:170
  364.2 17.0 %collective-permute-start.20 = (s16[64,4864]{1,0:T(8,128)(2,1)}, s16[64,4864]{1,0:T(8,128)(2,1)S(1)}, u32[]{:S(2)}, u32[]{:S(2)}) collective-permute-start(s16[64,4864]{1,0:T(8,128)(2,1)} %pad_add_fusion.15), channel_id=1, source_target_pairs={{4,0},{8,4},{12,8},{5,1},{9,5},{13,9},{6,2},{10,6},{14,10},{7,3},{... | collective-permute-start | bytes 1867784 | tf_op jit(solution)/shard_map/ppermute | solution.py:170
  365.6 12.3 %collective-permute-start.19 = (s16[64,4864]{1,0:T(8,128)(2,1)S(1)}, s16[64,4864]{1,0:T(8,128)(2,1)}, u32[]{:S(2)}, u32[]{:S(2)}) collective-permute-start(s16[64,4864]{1,0:T(8,128)(2,1)S(1)} %pad_add_fusion.14), channel_id=1, source_target_pairs={{0,4},{4,8},{8,12},{1,5},{5,9},{9,13},{2,6},{6,10},{10,14},{3,7},{... | collective-permute-start | bytes 1867784 | tf_op jit(solution)/shard_map/ppermute | solution.py:170
  391.3 18.3 %collective-permute-start.22 = (s16[64,4864]{1,0:T(8,128)(2,1)}, s16[64,4864]{1,0:T(8,128)(2,1)S(1)}, u32[]{:S(2)}, u32[]{:S(2)}) collective-permute-start(s16[64,4864]{1,0:T(8,128)(2,1)} %pad_add_fusion.17), channel_id=1, source_target_pairs={{4,0},{8,4},{12,8},{5,1},{9,5},{13,9},{6,2},{10,6},{14,10},{7,3},{... | collective-permute-start | bytes 1867784 | tf_op jit(solution)/shard_map/ppermute | solution.py:170
  392.7 13.6 %collective-permute-start.21 = (s16[64,4864]{1,0:T(8,128)(2,1)S(1)}, s16[64,4864]{1,0:T(8,128)(2,1)}, u32[]{:S(2)}, u32[]{:S(2)}) collective-permute-start(s16[64,4864]{1,0:T(8,128)(2,1)S(1)} %pad_add_fusion.16), channel_id=1, source_target_pairs={{0,4},{4,8},{8,12},{1,5},{5,9},{9,13},{2,6},{6,10},{10,14},{3,7},{... | collective-permute-start | bytes 1867784 | tf_op jit(solution)/shard_map/ppermute | solution.py:170
  421.5 22.0 %collective-permute-start.23 = (s16[64,4864]{1,0:T(8,128)(2,1)}, s16[64,4864]{1,0:T(8,128)(2,1)}, u32[]{:S(2)}, u32[]{:S(2)}) collective-permute-start(s16[64,4864]{1,0:T(8,128)(2,1)} %pad_add_fusion.18), channel_id=1, source_target_pairs={{0,4},{4,8},{8,12},{1,5},{5,9},{9,13},{2,6},{6,10},{10,14},{3,7},{... | collective-permute-start | bytes 1867784 | tf_op jit(solution)/shard_map/ppermute | solution.py:170
  (72 other events, 481.0 us)
Sparse Core Ops, SparseCore 0:
  642.2 65.0 reduce-scatter.1
